TPU v7x, 32 devices: a whole 2x2x4 slice. The times are simulated.
32 devices in a mesh: dp: 8 (over z, x), head: 4 (over y, core).
Axes of the slice: x: 2, y: 2, z: 4, core: 2. Of those that a mesh axis runs over, the one named last changes fastest.
Arguments:
- token_ids: int32 [2, 4096], P(None, ('dp', 'head')), may hold values from 0 to 31999
- lengths: int32 [2, 8, 3], P(None, 'dp'), may hold values from 1 to 409, 512 in all within a row
- valid: int32 [2, 4096], P(None, ('dp', 'head')), may hold values 0 or 1
- vocab_ids: int32 [4096], replicated, may hold values from 0 to 31999, as said below
- teacher: bfloat16 [2, 4096, 4096], P(None, ('dp', 'head')), may hold values from -12 to 12
- block: float32 [768, 12288], P(None, ('dp', 'head'))
- block_m: float32 [768, 12288], P(None, ('dp', 'head')), may hold values from -2.3841858e-07 to 2.3841858e-07
- block_v: float32 [768, 12288], P(None, ('dp', 'head')), may hold values from 1.1876942e-15 to 4.750777e-15
- bases: float32 [4, 768, 768], replicated
- table: float32 [32000, 768], P('dp'), may hold values from -0.4375 to 0.4375
- table_m: float32 [32000, 768], P('dp'), may hold values from -2.3841858e-07 to 2.3841858e-07
- table_v: float32 [32000, 768], P('dp'), may hold values from 1.1876942e-15 to 4.750777e-15
- gains: float32 [3, 768], replicated, may hold values from 0.5 to 1.5
- gains_m: float32 [3, 768], replicated, may hold values from -9.536743e-07 to 9.536743e-07
- gains_v: float32 [3, 768], replicated, may hold values from 1.899135e-14 to 7.6141784e-14
Outputs:
- loss: float32 [], replicated
- grad_norm: float32 [], replicated
- block_new: float32 [768, 12288], P(None, ('dp', 'head'))
- block_m_new: float32 [768, 12288], P(None, ('dp', 'head'))
- block_v_new: float32 [768, 12288], P(None, ('dp', 'head'))
- table_new: float32 [32000, 768], P('dp')
- table_m_new: float32 [32000, 768], P('dp')
- table_v_new: float32 [32000, 768], P('dp')
- gains_new: float32 [3, 768], replicated
- gains_m_new: float32 [3, 768], replicated
- gains_v_new: float32 [3, 768], replicated
- block_low: bfloat16 [768, 12288], P(None, ('dp', 'head'))
- table_low: bfloat16 [32000, 768], P('dp')
Inputs may be any that keep to these rules, and one draw needn't show every extreme that they name: `vocab_ids`: distinct ids. Each row holds the lengths of 3 sequences packed in order into one bucket; they sum to 512 and the largest is exactly 409.
All inputs are finite; a program needn't handle non-finite values. No bound on the sum of `valid` on one device may be relied on, other than what follows from the above.
Results may differ from a plain program's by a relative error of at most 0.02.
Values may be sent and summed in bfloat16 or wider, within the bound.
A program may use at most 248 MiB of HBM per device.

v0:
```python
import math
import jax
import jax.numpy as jnp
from jax import lax
from jax.sharding import PartitionSpec as P

D = 768
H = 12
HD = 64
FF = 3072
TOPV = 4096
STEP = 5
low = jnp.bfloat16
scale = HD ** (-0.5)
eps_norm = 1e-05
clip_norm = 0.002
beta_one = 0.9
beta_two = 0.99
adam_eps = 1e-08
decay_rate = 0.1
rate_block = 0.03
rate_table = 0.05
rate_gain = 0.4


def product(left, right):
    return jnp.dot(left, right, preferred_element_type=jnp.float32)


def contract_rows(left, right):
    return lax.dot_general(
        left, right, (((0,), (0,)), ((), ())), preferred_element_type=jnp.float32
    )


def contract_cols(left, right):
    return lax.dot_general(
        left, right, (((1,), (1,)), ((), ())), preferred_element_type=jnp.float32
    )


def rms_norm(value, gain):
    return value * lax.rsqrt(jnp.mean(value * value, axis=-1, keepdims=True) + eps_norm) * gain


def rms_back(value, gain, grad):
    r = lax.rsqrt(jnp.mean(value * value, axis=-1, keepdims=True) + eps_norm)
    scaled = grad * gain
    d_value = r * scaled - value * (r * r * r) * jnp.mean(value * scaled, axis=-1, keepdims=True)
    return (d_value, jnp.sum(grad * value * r, axis=0))


def rotary(value, cosine, sine):
    half = HD // 2
    turned = jnp.concatenate([-value[..., half:], value[..., :half]], axis=-1)
    return value * cosine[:, None, :] + turned * sine[:, None, :]


def rotary_back(grad, cosine, sine):
    half = HD // 2
    part = grad * sine[:, None, :]
    turned = jnp.concatenate([part[..., half:], -part[..., :half]], axis=-1)
    return grad * cosine[:, None, :] + turned


def segments(lengths, places):
    segment = jnp.zeros_like(places)
    begin = jnp.zeros_like(places)
    end = jnp.zeros((), jnp.int32)
    for index in range(lengths.shape[0] - 1):
        end = end + lengths[index]
        past = places >= end
        segment = segment + past.astype(jnp.int32)
        begin = jnp.where(past, end, begin)
    return (segment, places - begin)


def scores_of(query, keys, allow):
    score = jnp.einsum("qhd,khd->hqk", query, keys, preferred_element_type=jnp.float32) * scale
    return jnp.where(allow[None], score, -1e30)


def attend(query, keys, values, allow):
    score = scores_of(query, keys, allow)
    summit = jnp.max(score, axis=-1, keepdims=True)
    log_total = summit + jnp.log(jnp.sum(jnp.exp(score - summit), axis=-1, keepdims=True))
    weight = jnp.exp(score - log_total)
    mixed = jnp.einsum(
        "hqk,khd->qhd", weight.astype(low), values, preferred_element_type=jnp.float32
    )
    return (mixed.astype(low), log_total)


def attend_back(query, keys, values, log_total, upstream, allow):
    weight = jnp.exp(scores_of(query, keys, allow) - log_total)
    d_value = jnp.einsum(
        "hqk,qhd->khd", weight.astype(low), upstream, preferred_element_type=jnp.float32
    )
    d_weight = jnp.einsum("qhd,khd->hqk", upstream, values, preferred_element_type=jnp.float32)
    d_score = (weight * (d_weight - jnp.sum(d_weight * weight, axis=-1, keepdims=True))).astype(low)
    d_query = jnp.einsum("hqk,khd->qhd", d_score, keys, preferred_element_type=jnp.float32) * scale
    d_key = jnp.einsum("hqk,qhd->khd", d_score, query, preferred_element_type=jnp.float32) * scale
    return (d_query, d_key, d_value)


def swap(value, head_count, offset):
    return lax.ppermute(value, "head", [(h, h ^ offset) for h in range(head_count)])


def layer_forward(hidden, weights, gains, cosine, sine, allow, head_count):
    w_qkv, w_out, w_gu, w_down = weights
    rows = hidden.shape[0]
    normed = rms_norm(hidden, gains[0]).astype(low)
    qkv = contract_cols(normed, w_qkv).reshape(rows, 3, H, HD)
    query = rotary(qkv[:, 0], cosine, sine).astype(low)
    key = rotary(qkv[:, 1], cosine, sine).astype(low)
    own = jnp.concatenate([key, qkv[:, 2].astype(low)], axis=1)
    both = jnp.concatenate([own, swap(own, head_count, 1)], axis=0)
    keys, values = (both[:, :H], both[:, H:])
    mixed, log_total = attend(query, keys, values, allow)
    merged = mixed.reshape(rows, D)
    middle = hidden + contract_cols(merged, w_out)
    normed_two = rms_norm(middle, gains[1]).astype(low)
    gate_up = contract_cols(normed_two, w_gu)
    action = (jax.nn.silu(gate_up[:, :FF]) * gate_up[:, FF:]).astype(low)
    output = middle + product(action, w_down)
    saved = (
        hidden,
        normed,
        query,
        keys,
        values,
        log_total,
        merged,
        middle,
        normed_two,
        gate_up,
        action,
    )
    return (output, saved)


def layer_backward(gradient, weights, gains, saved, cosine, sine, allow, head_count):
    w_qkv, w_out, w_gu, w_down = weights
    hidden, normed, query, keys, values, log_total, merged, middle, normed_two, gate_up, action = (
        saved
    )
    rows = hidden.shape[0]
    grad_low = gradient.astype(low)
    d_down = contract_rows(action, grad_low)
    d_action = contract_cols(grad_low, w_down)
    gate, up = (gate_up[:, :FF], gate_up[:, FF:])
    chance = jax.nn.sigmoid(gate)
    d_gate = d_action * up * (chance + gate * chance * (1.0 - chance))
    d_up = d_action * gate * chance
    d_gate_up = jnp.concatenate([d_gate, d_up], axis=1).astype(low)
    d_gu = contract_rows(d_gate_up, normed_two)
    d_middle, d_gain_two = rms_back(middle, gains[1], product(d_gate_up, w_gu))
    d_middle = gradient + d_middle
    middle_low = d_middle.astype(low)
    d_out = contract_rows(middle_low, merged)
    upstream = product(middle_low, w_out).astype(low).reshape(rows, H, HD)
    d_query, d_key, d_value = attend_back(query, keys, values, log_total, upstream, allow)
    d_own = jnp.concatenate([d_key[:rows], d_value[:rows]], axis=1)
    d_far = jnp.concatenate([d_key[rows:], d_value[rows:]], axis=1).astype(low)
    d_own = (d_own + swap(d_far, head_count, 1).astype(jnp.float32)).astype(low).astype(jnp.float32)
    d_query = rotary_back(d_query.astype(low).astype(jnp.float32), cosine, sine)
    d_key = rotary_back(d_own[:, :H], cosine, sine)
    d_qkv = jnp.concatenate([d_query, d_key, d_own[:, H:]], axis=1).reshape(rows, 3 * D).astype(low)
    d_qkv_w = contract_rows(d_qkv, normed)
    d_hidden, d_gain_one = rms_back(hidden, gains[0], product(d_qkv, w_qkv))
    return (d_middle + d_hidden, [d_qkv_w, d_out, d_gu, d_down], d_gain_one, d_gain_two)


def adam_step(weight, gradient, first, second, rate, decay):
    first_new = beta_one * first + (1.0 - beta_one) * gradient
    second_new = beta_two * second + (1.0 - beta_two) * gradient * gradient
    direction = (
        first_new
        / (1.0 - beta_one**STEP)
        / (jnp.sqrt(second_new / (1.0 - beta_two**STEP)) + adam_eps)
    )
    return (weight - rate * (direction + decay * weight), first_new, second_new)


def on_device(
    token_ids,
    lengths,
    valid,
    vocab_ids,
    teacher,
    block,
    block_m,
    block_v,
    bases,
    table,
    table_m,
    table_v,
    gains,
    gains_m,
    gains_v,
):
    dp_count, head_count = (lax.axis_size("dp"), lax.axis_size("head"))
    device_total = dp_count * head_count
    head, dp = (lax.axis_index("head"), lax.axis_index("dp"))
    batch = head // 2
    tokens = token_ids.shape[1]
    shard_rows = table.shape[0]
    offset = dp * shard_rows
    part = TOPV // device_total
    codes = lax.all_gather(token_ids * 2 + valid, ("dp", "head"), axis=1, tiled=True)
    count = jnp.sum(codes & 1).astype(jnp.float32)
    codes = lax.dynamic_index_in_dim(codes, batch, 0, keepdims=False).reshape(
        dp_count, head_count, tokens
    )
    first = lax.dynamic_index_in_dim(codes, head, 1, keepdims=False)
    second = lax.dynamic_index_in_dim(codes, head ^ 2, 1, keepdims=False)
    codes = jnp.concatenate([first, second], axis=1)
    weighting = (lax.dynamic_index_in_dim(codes, dp, 0, keepdims=False) & 1).astype(jnp.float32)
    vocab = lax.dynamic_index_in_dim(
        vocab_ids.reshape(dp_count, head_count, part), head, 1, keepdims=False
    )
    local = jnp.concatenate([vocab, codes >> 1], axis=1) - offset
    owned = (local >= 0) & (local < shard_rows)
    rows_out = jnp.where(owned[..., None], table[jnp.clip(local, 0, shard_rows - 1)], 0.0).astype(
        low
    )
    rows_in = lax.psum_scatter(rows_out, "dp", scatter_dimension=0, tiled=True)
    rows_in = rows_in.reshape(part + 2 * tokens, D)
    chosen = lax.all_gather(rows_in[:part], ("dp", "head"), axis=0, tiled=True)
    hidden = rows_in[part:].astype(jnp.float32)
    widths = [3 * D // device_total, D // device_total, 2 * FF // device_total, FF // device_total]
    cuts = [sum(widths[:index]) for index in range(5)]
    gathered = lax.all_gather(block.T.astype(low), ("dp", "head"), axis=0)
    weights = [gathered[:, cuts[index] : cuts[index + 1]].reshape(-1, D) for index in range(4)]
    teacher_own = lax.dynamic_index_in_dim(teacher, batch, 0, keepdims=False)
    teacher_far = swap(
        lax.dynamic_index_in_dim(teacher, 1 - batch, 0, keepdims=False), head_count, 2
    )
    teacher_rows = jnp.concatenate([teacher_own, teacher_far], axis=0)
    run = jnp.arange(tokens, dtype=jnp.int32)
    places = jnp.concatenate([head * tokens + run, (head ^ 2) * tokens + run])
    places_far = jnp.concatenate([(head ^ 1) * tokens + run, (head ^ 3) * tokens + run])
    own_lengths = lax.dynamic_index_in_dim(lengths, batch, 0, keepdims=False)[0]
    segment, position = segments(own_lengths, places)
    segment_far, unused = segments(own_lengths, places_far)
    places_all = jnp.concatenate([places, places_far])
    segment_all = jnp.concatenate([segment, segment_far])
    allow = (segment[:, None] == segment_all[None, :]) & (places[:, None] >= places_all[None, :])
    freqs = jnp.exp(jnp.arange(0, HD, 2, dtype=jnp.float32) * (-math.log(10000.0) / HD))
    angle = position.astype(jnp.float32)[:, None] * freqs[None, :]
    angle = jnp.concatenate([angle, angle], axis=1)
    cosine, sine = (jnp.cos(angle), jnp.sin(angle))
    saves = []
    for repeat in range(2):
        hidden, saved = layer_forward(hidden, weights, gains, cosine, sine, allow, head_count)
        saves.append(saved)
    normed = rms_norm(hidden, gains[2]).astype(low)
    log_prob = jax.nn.log_softmax(contract_cols(normed, chosen), axis=-1)
    teach = jax.nn.log_softmax(teacher_rows.astype(jnp.float32), axis=-1)
    loss_sum = jnp.sum(weighting * jnp.sum(jnp.exp(teach) * (teach - log_prob), axis=-1))
    logit_grads = ((jnp.exp(log_prob) - jnp.exp(teach)) * weighting[:, None]).astype(low)
    chosen_grads = contract_rows(logit_grads, normed).astype(low)
    gradient, d_gain_final = rms_back(hidden, gains[2], product(logit_grads, chosen))
    chosen_grads = lax.psum_scatter(chosen_grads, ("dp", "head"), scatter_dimension=0, tiled=True)
    block_grads = None
    d_gains = [0.0, 0.0]
    for repeat in range(2):
        gradient, layer_grads, d_gain_one, d_gain_two = layer_backward(
            gradient, weights, gains, saves[1 - repeat], cosine, sine, allow, head_count
        )
        d_gains = [d_gains[0] + d_gain_one, d_gains[1] + d_gain_two]
        if block_grads is None:
            block_grads = layer_grads
        else:
            block_grads = [total + extra for total, extra in zip(block_grads, layer_grads)]
    joined = jnp.concatenate(
        [piece.astype(low).reshape(device_total, -1, D) for piece in block_grads], axis=1
    )
    block_grads = lax.psum_scatter(joined, ("dp", "head"), scatter_dimension=0, tiled=True)
    block_grads = block_grads.reshape(-1, D).astype(jnp.float32).T
    rows_back = jnp.concatenate([chosen_grads, gradient.astype(low)], axis=0)
    rows_back = lax.all_gather(rows_back, "dp", axis=0, tiled=True)
    dump_index = jnp.where(owned, local, shard_rows).reshape(-1)
    table_grads = jax.ops.segment_sum(
        rows_back.astype(jnp.float32), dump_index, num_segments=shard_rows + 1
    )[:shard_rows]
    table_grads = lax.psum(table_grads.astype(low), "head").astype(jnp.float32)
    small = jnp.concatenate([d_gains[0], d_gains[1], d_gain_final, loss_sum[None]])
    small = lax.psum(small, ("dp", "head"))
    gain_grads = small[: 3 * D].reshape(3, D) / count
    loss = small[3 * D] / count
    squares = lax.psum(
        jnp.sum(block_grads * block_grads)
        + jnp.where(head == 0, jnp.sum(table_grads * table_grads), 0.0),
        ("dp", "head"),
    )
    grad_norm = jnp.sqrt(squares / (count * count) + jnp.sum(gain_grads * gain_grads))
    clip = jnp.minimum(1.0, clip_norm / grad_norm)
    factor = clip / count
    block_grads = block_grads * factor
    table_grads = table_grads * factor
    gain_grads = gain_grads * clip
    rotated = jnp.concatenate(
        [
            contract_rows(bases[index], block_grads[:, cuts[index] : cuts[index + 1]])
            for index in range(4)
        ],
        axis=1,
    )
    block_m_new = beta_one * block_m + (1.0 - beta_one) * rotated
    block_v_new = beta_two * block_v + (1.0 - beta_two) * rotated * rotated
    direction = (
        block_m_new
        / (1.0 - beta_one**STEP)
        / (jnp.sqrt(block_v_new / (1.0 - beta_two**STEP)) + adam_eps)
    )
    update = jnp.concatenate(
        [product(bases[index], direction[:, cuts[index] : cuts[index + 1]]) for index in range(4)],
        axis=1,
    )
    block_new = block - rate_block * (update + decay_rate * block)
    table_new, table_m_new, table_v_new = adam_step(
        table, table_grads, table_m, table_v, rate_table, decay_rate
    )
    gains_new, gains_m_new, gains_v_new = adam_step(
        gains, gain_grads, gains_m, gains_v, rate_gain, 0.0
    )
    return (
        loss,
        grad_norm,
        block_new,
        block_m_new,
        block_v_new,
        table_new,
        table_m_new,
        table_v_new,
        gains_new,
        gains_m_new,
        gains_v_new,
        block_new.astype(low),
        table_new.astype(low),
    )


def solution(mesh):
    tokens = P(None, ("dp", "head"))
    columns = P(None, ("dp", "head"))
    table = P("dp", None)
    return jax.shard_map(
        on_device,
        mesh=mesh,
        in_specs=(
            tokens,
            P(None, "dp", None),
            tokens,
            P(),
            P(None, ("dp", "head"), None),
            columns,
            columns,
            columns,
            P(),
            table,
            table,
            table,
            P(),
            P(),
            P(),
        ),
        out_specs=(
            P(),
            P(),
            columns,
            columns,
            columns,
            table,
            table,
            table,
            P(),
            P(),
            P(),
            columns,
            table,
        ),
        check_vma=False,
    )
```

profile of v0, /device:TPU:0, one launch (start us, length us, event | category | flops | bytes accessed | tf_op | source)
XLA Modules:
  0.0 969.5 jit_solution(10707794897695880077)
XLA Ops:
  8.8 43.2 %all_gather.15 = s32[2,4096]{1,0:T(2,128)S(1)} all-gather(s32[2,128]{1,0:T(2,128)S(1)} %multiply_add_fusion.2), channel_id=1, replica_groups=mesh['dp'=8,'head'=4] {'dp','head'}, dimensions={1}, use_global_device_ids=true | all-gather | bytes 33792 | tf_op jit(solution)/shard_map/all_gather | solution.py:211
  53.4 19.0 %gather_fusion = bf16[3072,768]{1,0:T(8,128)(2,1)} fusion(f32[4000,768]{1,0:T(8,128)} %param.25, s32[3072]{0:T(1024)S(1)} %broadcast_clamp_fusion), kind=kCustom, calls=%fused_computation | custom fusion | bytes 9449472 | tf_op jit(solution)/shard_map/gather | solution.py:225
  72.5 5.8 select_convert_fusion
  85.2 155.6 %reduce-scatter.4.cloned.1.call-done = bf16[1,384,768]{2,1,0:T(8,128)(2,1)} async-done(((bf16[8,384,768]{2,1,0:T(8,128)(2,1)}), bf16[1,384,768]{2,1,0:T(8,128)(2,1)}) %reduce-scatter.4.cloned.1.call-update) | async-done | bytes 589840 | tf_op jit(solution)/shard_map/reduce_scatter | solution.py:228
  242.5 24.5 %copy.41 = bf16[12288,768]{1,0:T(8,128)(2,1)} copy(bf16[12288,768]{0,1:T(8,128)(2,1)} %all-gather.8.cloned.1.call-done) | data formatting | bytes 37748736 | tf_op jit(solution)/shard_map/all_gather | solution.py:234
  267.1 2.3 slice.311
  281.2 2.4 slice.320
  283.6 8.4 slice.321
  292.0 4.9 slice.324
  299.7 2.0 exponential_reduce_fusion.1
  302.3 3.5 convolution_convert_fusion.2
  307.1 2.7 fusion.177
  312.5 4.4 multiply_reduce_fusion.12
  324.2 2.1 fusion.22
  329.8 2.2 exponential_reduce_fusion
  333.0 3.7 convolution_convert_fusion.1
  337.4 2.7 fusion.179
  342.8 5.2 multiply_reduce_fusion.10
  348.0 2.0 all-gather.10.cloned.1.call-done
  350.0 5.0 fusion.192
  355.8 4.2 fusion.20
  360.0 2.6 multiply_reduce_fusion.9
  362.9 2.4 multiply_convert_fusion.5
  365.6 3.4 multiply_reduce_fusion.8
  371.4 1.9 copy.42
  373.4 4.6 convolution_bitcast_fusion.1
  378.0 2.4 multiply_reduce_fusion.1
  380.5 1.8 multiply_convert_fusion.1
  386.3 4.7 convolution_convert_fusion
  391.1 2.2 slice-done.23
  395.1 2.2 broadcast_multiply_fusion.1
  398.1 2.0 copy-done.5
  400.3 1.9 multiply_reduce_fusion.7
  402.6 2.8 multiply_convert_fusion.3
  405.7 3.4 multiply_reduce_fusion.5
  412.7 4.4 convolution_bitcast_fusion
  417.6 2.4 multiply_reduce_fusion
  420.0 1.8 multiply_convert_fusion
  423.2 1.9 collective-permute-done.4
  425.3 2.1 broadcast_multiply_fusion
  428.0 2.1 copy-done.6
  430.3 1.9 fusion.102
  432.5 71.6 %reduce-scatter.8.cloned.1.call-done = bf16[128,768]{1,0:T(8,128)(2,1)} async-done(((bf16[4096,768]{1,0:T(8,128)(2,1)}), bf16[128,768]{1,0:T(8,128)(2,1)}) %reduce-scatter.8.cloned.1.call-update) | async-done | bytes 196624 | tf_op jit(solution)/shard_map/reduce_scatter | solution.py:265
  504.1 1.8 pad_maximum_fusion.16
  510.6 8.2 fusion.50
  520.8 3.7 add_convert_fusion.1
  524.5 11.0 %add_convert_fusion = bf16[6144,768]{1,0:T(8,128)(2,1)} fusion(f32[6144,768]{1,0:T(8,128)} %fusion.50, bf16[256,3072]{1,0:T(8,128)(2,1)} %copy-done.91, bf16[256,3072]{1,0:T(8,128)(2,1)S(1)} %copy-done.90, f32[256,768]{1,0:T(8,128)S(1)} %copy-done.14, f32[768]{0:T(1024)S(1)} %get-tuple-element.51, f32[256]{0:T(256)S(1)} %copy-done.112), kind=kOutput, calls=%fused_computation.3 | convolution fusion | flops 2432237568 | bytes 32247808 | tf_op jit(solution)/shard_map/dot_general | solution.py:31
  535.5 49.3 %all-gather.6.cloned.1.call-done = bf16[3072,768]{1,0:T(8,128)(2,1)} async-done(((bf16[384,768]{1,0:T(8,128)(2,1)}), bf16[3072,768]{1,0:T(8,128)(2,1)}) %all-gather.6.cloned.1.call-update) | async-done | bytes 4718608 | tf_op jit(solution)/shard_map/all_gather | solution.py:283
  584.9 26.8 %scatter_custom_fusion = f32[4001,768]{1,0:T(8,128)} fusion(s32[3072]{0:T(1024)S(1)} %bitcast.297, bf16[3072,768]{1,0:T(8,128)(2,1)} %all-gather.6.cloned.1.call-done, f32[]{:T(128)} %constant.61.clone.1), kind=kCustom, calls=%fused_computation.13 | custom fusion | flops 4718592 | bytes 17009668 | tf_op jit(solution)/shard_map/scatter-add | solution.py:285
  611.7 7.7 slice.532
  623.8 15.2 %pad_maximum_fusion = bf16[32,384,768]{2,1,0:T(8,128)(2,1)} fusion(bf16[32,96,768]{2,1,0:T(8,128)(2,1)} %bitcast.265, bf16[32,192,768]{2,1,0:T(8,128)(2,1)} %bitcast.245, bf16[32,24,768]{2,1,0:T(8,128)(2,1)S(1)} %bitcast.271, bf16[32,72,768]{2,1,0:T(8,128)(2,1)S(1)} %bitcast.266), kind=kLoop, calls=%fused_computation.2 | loop fusion | flops 75497472 | bytes 37748736 | tf_op jit(solution)/shard_map/concatenate | solution.py:277
  646.5 97.7 %all-reduce.3.cloned.1.call-done = bf16[4000,768]{1,0:T(8,128)(2,1)} async-done(((bf16[4000,768]{1,0:T(8,128)(2,1)}), bf16[4000,768]{1,0:T(8,128)(2,1)}) %all-reduce.3.cloned.1.call-update) | async-done | bytes 6144016 | tf_op jit(solution)/shard_map/psum | solution.py:288
  744.2 6.6 fusion.2
  751.5 106.8 %reduce-scatter.6.cloned.1.call-done = bf16[1,384,768]{2,1,0:T(8,128)(2,1)} async-done(((bf16[32,384,768]{2,1,0:T(8,128)(2,1)}), bf16[1,384,768]{2,1,0:T(8,128)(2,1)}) %reduce-scatter.6.cloned.1.call-update) | async-done | bytes 589840 | tf_op jit(solution)/shard_map/reduce_scatter | solution.py:280
  858.3 2.0 fusion.66
  860.9 39.9 %all-reduce = (f32[2305]{0:T(1024)S(1)}, f32[]{:T(128)}) all-reduce(f32[2305]{0:T(1024)S(1)} %pad_maximum_fusion.18, f32[]{:T(128)S(6)} %add.365), channel_id=1, replica_groups=mesh['dp'=8,'head'=4] {'dp','head'}, use_global_device_ids=true, to_apply=%region_25.27 | all-reduce | flops 2306 | bytes 18448 | tf_op jit(solution)/shard_map/psum | solution.py:290
  904.5 2.2 fusion.71
  906.7 2.1 fusion.60
  908.8 2.0 fusion.83
  910.8 2.2 fusion.77
  912.9 2.2 add_divide_fusion.2
  920.7 2.8 fusion.183
  923.5 2.8 copy.48
  930.8 28.9 %fusion.180 = (bf16[4000,768]{1,0:T(8,128)(2,1)}, f32[4000,768]{1,0:T(8,128)}, f32[4000,768]{1,0:T(8,128)}, f32[4000,768]{1,0:T(8,128)}) fusion(f32[4000,768]{1,0:T(8,128)} %param.25, f32[]{:T(128)S(6)} %div.137, bf16[4000,768]{1,0:T(8,128)(2,1)} %all-reduce.3.cloned.1.call-done, f32[4000,768]{1,0:T(8,128)} %param.26, f32[4000,768]{1,0:T(8,128)} %param.27), kind=kLoop, calls=%fused_computation.347 | loop fusion | flops 55296000 | bytes 86016000 | tf_op jit(solution)/shard_map/convert_element_type | solution.py:342
  (488 shorter events, 90.2 us)
Async XLA Ops:
  8.0 72.6 %copy-start = (s32[2,1,3]{2,1,0:T(1,128)S(1)}, s32[2,1,3]{2,1,0:T(1,128)}, u32[]{:S(2)}) copy-start(s32[2,1,3]{2,1,0:T(1,128)} %param.17) | copy-start | bytes 76
  8.0 232.8 %reduce-scatter.4.cloned.1.call-start = ((), (), s32[]{:S(2)}) async-start(), calls=%async_computation.3 | async-start | bytes 5308416 | tf_op jit(solution)/shard_map/reduce_scatter | solution.py:228
  52.0 20.4 %copy-start.95 = (s32[2,4096]{1,0:T(2,128)}, s32[2,4096]{1,0:T(2,128)S(1)}, u32[]{:S(2)}) copy-start(s32[2,4096]{1,0:T(2,128)S(1)} %all_gather.15) | copy-start | bytes 98308
  52.8 19.7 %copy-start.103 = (s32[8,1,128]{2,1,0:T(1,128)}, s32[8,1,128]{2,1,0:T(1,128)S(1)}, u32[]{:S(2)}) copy-start(s32[8,1,128]{2,1,0:T(1,128)S(1)} %get-tuple-element.156) | copy-start | bytes 12292
  52.8 19.6 %copy-start.101 = (s32[8,256]{1,0:T(8,128)}, s32[8,256]{1,0:T(8,128)S(1)}, u32[]{:S(2)}) copy-start(s32[8,256]{1,0:T(8,128)S(1)} %get-tuple-element.112) | copy-start | bytes 24580
  78.3 5.9 copy-start.105
  78.4 164.2 %all-gather.8.cloned.1.call-start = ((), (), s32[]{:S(2)}) async-start(), calls=%async_computation.8 | async-start | bytes 19464192 | tf_op jit(solution)/shard_map/all_gather | solution.py:234
  80.5 269.5 %all-gather.10.cloned.1.call-start = ((), (), s32[]{:S(2)}) async-start(), calls=%async_computation.9 | async-start | bytes 6488064 | tf_op jit(solution)/shard_map/all_gather | solution.py:230
  83.1 184.0 %copy-start.136 = (s32[128]{0:T(128)}, s32[128]{0:T(128)S(1)}, u32[]{:S(2)}) copy-start(s32[128]{0:T(128)S(1)} %iota_add_fusion.3) | copy-start | bytes 1540
  269.4 48.3 %copy-start.4 = (bf16[32,72,768]{2,1,0:T(8,128)(2,1)}, bf16[32,72,768]{2,1,0:T(8,128)(2,1)S(1)}, u32[]{:S(2)}) copy-start(bf16[32,72,768]{2,1,0:T(8,128)(2,1)S(1)} %slice.311) | copy-start | bytes 10616836
  273.6 23.3 %collective-permute-start = (bf16[256,24,64]{0,2,1:T(8,128)(2,1)}, bf16[256,24,64]{0,2,1:T(8,128)(2,1)}, u32[]{:S(2)}, u32[]{:S(2)}) collective-permute-start(bf16[256,24,64]{0,2,1:T(8,128)(2,1)} %pad_maximum_fusion.12), channel_id=1, source_target_pairs={{0,1},{1,0},{2,3},{3,2},{4,5},{5,4},{6,7},{7,6},{8,9},{9,8},{10,11... | collective-permute-start | bytes 2359304 | tf_op jit(solution)/shard_map/ppermute | solution.py:107
  275.2 47.4 %collective-permute-start.2 = (bf16[128,4096]{1,0:T(8,128)(2,1)}, bf16[128,4096]{1,0:T(8,128)(2,1)}, u32[]{:S(2)}, u32[]{:S(2)}) collective-permute-start(bf16[128,4096]{1,0:T(8,128)(2,1)} %get-tuple-element.82), channel_id=1, source_target_pairs={{0,2},{1,3},{2,0},{3,1},{4,6},{5,7},{6,4},{7,5},{8,10},{9,11},{10,... | collective-permute-start | bytes 3145736 | tf_op jit(solution)/shard_map/ppermute | solution.py:107
  281.2 222.9 %reduce-scatter.8.cloned.1.call-start = ((), (), s32[]{:S(2)}) async-start(), calls=%async_computation.5 | async-start | bytes 6488064 | tf_op jit(solution)/shard_map/reduce_scatter | solution.py:265
  292.0 4.9 copy-start.60
  292.0 4.9 copy-start.66
  301.7 5.4 slice-start
  306.4 6.1 copy-start.12
  318.9 8.0 copy-start.62
  321.1 5.8 copy-start.68
  321.2 5.8 collective-permute-start.1
  329.7 7.7 slice-start.3
  337.3 31.7 %copy-start.15 = (f32[256,768]{1,0:T(8,128)}, f32[256,768]{1,0:T(8,128)S(1)}, u32[]{:S(2)}) copy-start(f32[256,768]{1,0:T(8,128)S(1)} %get-tuple-element.138) | copy-start | bytes 2359300
  337.4 31.6 %copy-start.108 = (f32[256]{0:T(256)}, f32[256]{0:T(256)S(1)}, u32[]{:S(2)}) copy-start(f32[256]{0:T(256)S(1)} %get-tuple-element.121) | copy-start | bytes 3076
  342.8 5.2 copy-start.32
  348.0 14.6 %copy-start.121 = (f32[256]{0:T(256)}, f32[256]{0:T(256)S(1)}, u32[]{:S(2)}) copy-start(f32[256]{0:T(256)S(1)} %get-tuple-element.123) | copy-start | bytes 3076
  355.0 5.0 copy-start.75
  355.0 5.0 copy-start.137
  355.7 7.1 slice-start.21
  355.7 7.1 slice-start.24
  360.0 5.3 slice-start.6
  360.0 5.4 slice-start.7
  362.8 6.2 copy-start.40
  370.2 7.8 slice-start.14
  383.0 8.0 copy-start.50
  384.3 6.8 collective-permute-start.3
  391.0 11.5 %slice-start.26 = ((s8[4718592]{0:T(1024)(128)(4,1)}), s8[524288]{0:T(1024)(128)(4,1)S(1)}, s32[]{:S(2)}) async-start(s8[4718592]{0:T(1024)(128)(4,1)} %bitcast.277), calls=%async_computation.36 | async-start | bytes 1048576
  391.0 193.8 %all-gather.6.cloned.1.call-start = ((), (), s32[]{:S(2)}) async-start(), calls=%async_computation.6 | async-start | bytes 5308416 | tf_op jit(solution)/shard_map/all_gather | solution.py:283
  393.3 9.2 slice-start.19
  395.1 7.4 slice-start.20
  395.1 7.4 slice-start.27
  400.3 5.1 slice-start.9
  402.5 6.6 copy-start.42
  409.1 8.0 slice-start.12
  412.7 4.9 copy-start.45
  412.7 4.9 copy-start.98
  422.7 2.4 collective-permute-start.4
  432.2 73.9 %copy-start.102 = (s32[8,256]{1,0:T(8,128)S(1)}, s32[8,256]{1,0:T(8,128)}, u32[]{:S(2)}) copy-start(s32[8,256]{1,0:T(8,128)} %copy-done.101) | copy-start | bytes 24580
  432.2 74.7 %copy-start.25 = (f32[256,768]{1,0:T(8,128)S(1)}, f32[256,768]{1,0:T(8,128)}, u32[]{:S(2)}) copy-start(f32[256,768]{1,0:T(8,128)} %copy-done.23) | copy-start | bytes 2359300
  432.5 76.0 %copy-start.33 = (bf16[256,3072]{1,0:T(8,128)(2,1)S(1)}, bf16[256,3072]{1,0:T(8,128)(2,1)}, u32[]{:S(2)}) copy-start(bf16[256,3072]{1,0:T(8,128)(2,1)} %copy-done.32) | copy-start | bytes 4718596
  505.9 238.4 %all-reduce.3.cloned.1.call-start = ((), (), s32[]{:S(2)}) async-start(), calls=%async_computation.7 | async-start | bytes 12288000 | tf_op jit(solution)/shard_map/psum | solution.py:288
  510.6 8.2 copy-start.86
  619.5 238.8 %reduce-scatter.6.cloned.1.call-start = ((), (), s32[]{:S(2)}) async-start(), calls=%async_computation.4 | async-start | bytes 19464192 | tf_op jit(solution)/shard_map/reduce_scatter | solution.py:280
  640.4 4.8 copy-start.128
  640.4 5.4 copy-start.131
  640.4 5.4 copy-start.133
  640.4 5.4 copy-start.132
  640.4 5.4 copy-start.134
  640.4 5.4 copy-start.130
  744.2 170.9 %slice-start.16 = ((s8[9437184]{0:T(1024)(128)(4,1)}), s8[1048576]{0:T(1024)(128)(4,1)S(1)}, s32[]{:S(2)}) async-start(s8[9437184]{0:T(1024)(128)(4,1)} %bitcast.254), calls=%async_computation.26 | async-start | bytes 2097152
  904.5 10.6 %slice-start.17 = ((s8[9437184]{0:T(1024)(128)(4,1)}), s8[4194304]{0:T(1024)(128)(4,1)S(1)}, s32[]{:S(2)}) async-start(s8[9437184]{0:T(1024)(128)(4,1)} %bitcast.254), calls=%async_computation.27 | async-start | bytes 8388608
  920.7 5.6 copy-start.55
  923.5 5.6 copy-start.104
  923.5 5.6 copy-start.77
  930.8 28.9 %copy-start.1 = (s32[2,1,3]{2,1,0:T(1,128)S(1)}, s32[2,1,3]{2,1,0:T(1,128)}, u32[]{:S(2)}) copy-start(s32[2,1,3]{2,1,0:T(1,128)} %param.17) | copy-start | bytes 76
  (114 other events, 310.9 us)
Sparse Core Ops, SparseCore 0:
  78.5 162.2 reduce-scatter.3
  506.0 78.8 all-gather.5
  619.6 124.5 all-reduce.2
Sparse Core Ops, SparseCore 1:
  82.3 157.9 all-gather.7
  281.3 68.7 all-gather.9
  391.1 112.9 reduce-scatter.7
  639.1 219.1 reduce-scatter.5
where the time goes:
time: 978 us; the launch traced here: 970 us
  waiting for transfers between devices  485 us (50%)
  other arithmetic  139 us (14%)
  matrix products  121 us (12%)
  local copies, waits for them, and re-layouts  113 us (12%)
  blocking collectives  83.2 us (9%)
  between operations  25.5 us (3%)
    reduce_scatter x1, waiting for transfers between devices, on_device(): rows_in = lax.psum_scatter(rows_out, 'dp', scatter_dimension=0, tiled=True)  156 us
    reduce_scatter x1, waiting for transfers between devices, on_device(): lax.psum_scatter(joined, ('dp', 'head'), scatter_dimension=0, tiled=True)  107 us
    psum x1, waiting for transfers between devices, on_device(): table_grads = lax.psum(table_grads.astype(low), 'head').astype(jnp.float32)  97.7 us
    reduce_scatter x1, waiting for transfers between devices, on_device(): lax.psum_scatter(chosen_grads, ('dp', 'head'), scatter_dimension=0, tiled...  71.6 us
    all_gather x1, waiting for transfers between devices, on_device(): rows_back = lax.all_gather(rows_back, 'dp', axis=0, tiled=True)  49.3 us
    all_gather x1, blocking collectives, on_device(): lax.all_gather(token_ids * 2 + valid, ('dp', 'head'), axis=1, tiled=True)  43.2 us
    dot_general x13, matrix products, contract_rows(): lax.dot_general(left, right, (((0,), (0,)), ((), ())), preferred_element_...  42.8 us
    psum x1, blocking collectives, on_device(): small = lax.psum(small, ('dp', 'head'))  39.9 us
  transfers between devices with their start and end apart: 12, of which 7 were waited for; matrix products, arithmetic and copies ran while one was open for 17% of the time, Pallas kernels for 0%

commit v1 on v0

--- a/solution.py
+++ b/solution.py
@@ -285,7 +285,9 @@
     table_grads = jax.ops.segment_sum(
         rows_back.astype(jnp.float32), dump_index, num_segments=shard_rows + 1
     )[:shard_rows]
-    table_grads = lax.psum(table_grads.astype(low), "head").astype(jnp.float32)
+    table_grads = jnp.sum(lax.all_gather(table_grads.astype(low), "head"), axis=0).astype(
+        jnp.float32
+    )
     small = jnp.concatenate([d_gains[0], d_gains[1], d_gain_final, loss_sum[None]])
     small = lax.psum(small, ("dp", "head"))
     gain_grads = small[: 3 * D].reshape(3, D) / count

time: 978 us -> 1030 us (1.053)
  waiting for transfers between devices: 485 us -> 509 us
  other arithmetic: 139 us -> 155 us
    reduce_scatter x1, waiting for transfers between devices: 107 us -> 254 us  [on_device(): lax.psum_scatter(joined, ('dp', 'head'), scatter_dimension=0, tiled=True)]
    psum x1 -> x0, waiting for transfers between devices: 97.7 us -> none  [on_device(): table_grads = lax.psum(table_grads.astype(low), 'head').astype(jnp.float32)]
    all_gather x1, waiting for transfers between devices: 49.3 us -> 23.2 us  [on_device(): rows_back = lax.all_gather(rows_back, 'dp', axis=0, tiled=True)]
    reduce_sum x0 -> x1, other arithmetic: none -> 17.3 us  [on_device(): jnp.sum(lax.all_gather(table_grads.astype(low), 'head'), axis=0)]
    unnamed x338 -> x336, local copies, waits for them, and re-layouts: 31.5 us -> 30.1 us
  transfers between devices with their start and end apart: 12 -> 12, of which waited for: 7 -> 6; matrix products, arithmetic and copies ran while one was open for 17% -> 20% of each run, Pallas kernels for 0% -> 0%
where the time goes in v1:
time: 1030 us; the launch traced here: 1020 us
  waiting for transfers between devices  509 us (49%)
  other arithmetic  155 us (15%)
  matrix products  130 us (13%)
  local copies, waits for them, and re-layouts  112 us (11%)
  blocking collectives  83.2 us (8%)
  between operations  25.6 us (2%)
    reduce_scatter x1, waiting for transfers between devices, on_device(): lax.psum_scatter(joined, ('dp', 'head'), scatter_dimension=0, tiled=True)  254 us
    reduce_scatter x1, waiting for transfers between devices, on_device(): rows_in = lax.psum_scatter(rows_out, 'dp', scatter_dimension=0, tiled=True)  156 us
    reduce_scatter x1, waiting for transfers between devices, on_device(): lax.psum_scatter(chosen_grads, ('dp', 'head'), scatter_dimension=0, tiled...  71.6 us
    dot_general x13, matrix products, contract_rows(): lax.dot_general(left, right, (((0,), (0,)), ((), ())), preferred_element_...  52.1 us
    all_gather x1, blocking collectives, on_device(): lax.all_gather(token_ids * 2 + valid, ('dp', 'head'), axis=1, tiled=True)  43.2 us
    psum x1, blocking collectives, on_device(): small = lax.psum(small, ('dp', 'head'))  39.9 us
    unnamed x336, local copies, waits for them, and re-layouts  30.1 us
    dot_general x13, matrix products, product(): return jnp.dot(left, right, preferred_element_type=jnp.float32)  29.4 us
  transfers between devices with their start and end apart: 12, of which 6 were waited for; matrix products, arithmetic and copies ran while one was open for 20% of the time, Pallas kernels for 0%

profile of v1, /device:TPU:0, one launch (start us, length us, event | category | flops | bytes accessed | tf_op | source)
XLA Modules:
  0.0 1017.6 jit_solution(17755199458363452493)
XLA Ops:
  8.8 43.2 %all_gather.21 = s32[2,4096]{1,0:T(2,128)S(1)} all-gather(s32[2,128]{1,0:T(2,128)S(1)} %multiply_add_fusion.2), channel_id=1, replica_groups=mesh['dp'=8,'head'=4] {'dp','head'}, dimensions={1}, use_global_device_ids=true | all-gather | bytes 33792 | tf_op jit(solution)/shard_map/all_gather | solution.py:211
  53.4 19.0 %gather_fusion = bf16[3072,768]{1,0:T(8,128)(2,1)} fusion(f32[4000,768]{1,0:T(8,128)} %param.25, s32[3072]{0:T(1024)S(1)} %broadcast_clamp_fusion), kind=kCustom, calls=%fused_computation | custom fusion | bytes 9449472 | tf_op jit(solution)/shard_map/gather | solution.py:225
  72.5 5.8 select_convert_fusion
  85.2 155.6 %reduce-scatter.4.cloned.1.call-done = bf16[1,384,768]{2,1,0:T(8,128)(2,1)} async-done(((bf16[8,384,768]{2,1,0:T(8,128)(2,1)}), bf16[1,384,768]{2,1,0:T(8,128)(2,1)}) %reduce-scatter.4.cloned.1.call-update) | async-done | bytes 589840 | tf_op jit(solution)/shard_map/reduce_scatter | solution.py:228
  242.5 24.4 %copy.52 = bf16[12288,768]{1,0:T(8,128)(2,1)} copy(bf16[12288,768]{0,1:T(8,128)(2,1)} %all-gather.10.cloned.1.call-done) | data formatting | bytes 37748736 | tf_op jit(solution)/shard_map/all_gather | solution.py:234
  267.0 2.3 slice.311
  281.2 2.4 slice.320
  283.5 8.4 slice.321
  292.0 4.9 slice.324
  299.6 2.0 exponential_reduce_fusion.1
  302.3 3.3 convolution_convert_fusion.2
  306.9 2.7 fusion.177
  312.3 4.4 multiply_reduce_fusion.12
  324.1 2.1 fusion.22
  329.6 2.2 exponential_reduce_fusion
  332.8 3.7 convolution_convert_fusion.1
  337.3 2.7 fusion.179
  342.7 5.2 multiply_reduce_fusion.10
  347.9 2.0 all-gather.12.cloned.1.call-done
  349.9 5.0 fusion.192
  355.7 4.2 fusion.20
  359.9 2.6 multiply_reduce_fusion.9
  362.8 2.4 multiply_convert_fusion.5
  365.5 3.4 multiply_reduce_fusion.8
  371.3 1.9 copy.53
  373.3 4.6 convolution_bitcast_fusion.1
  377.9 2.4 multiply_reduce_fusion.1
  386.2 4.7 convolution_convert_fusion
  391.0 2.2 slice-done.23
  395.0 2.2 broadcast_multiply_fusion.1
  398.0 2.0 copy-done.5
  400.2 1.9 multiply_reduce_fusion.7
  402.5 2.8 multiply_convert_fusion.3
  405.6 3.4 multiply_reduce_fusion.5
  412.6 4.4 convolution_bitcast_fusion
  417.5 2.4 multiply_reduce_fusion
  423.1 1.9 collective-permute-done.4
  425.3 2.1 broadcast_multiply_fusion
  428.0 2.1 copy-done.6
  430.2 1.9 fusion.102
  432.4 71.6 %reduce-scatter.8.cloned.1.call-done = bf16[128,768]{1,0:T(8,128)(2,1)} async-done(((bf16[4096,768]{1,0:T(8,128)(2,1)}), bf16[128,768]{1,0:T(8,128)(2,1)}) %reduce-scatter.8.cloned.1.call-update) | async-done | bytes 196624 | tf_op jit(solution)/shard_map/reduce_scatter | solution.py:265
  509.8 8.3 fusion.50
  519.7 4.1 fusion.178
  523.9 3.7 add_convert_fusion.1
  527.6 11.5 %add_convert_fusion = bf16[6144,768]{1,0:T(8,128)(2,1)} fusion(f32[6144,768]{1,0:T(8,128)} %fusion.50, bf16[256,3072]{1,0:T(8,128)(2,1)} %copy-done.90, bf16[256,3072]{1,0:T(8,128)(2,1)} %copy-done.89, f32[256,768]{1,0:T(8,128)S(1)} %copy-done.15, f32[768]{0:T(1024)S(1)} %get-tuple-element.64, f32[256]{0:T(256)S(1)} %copy-done.109), kind=kOutput, calls=%fused_computation.3 | convolution fusion | flops 2432237568 | bytes 32247808 | tf_op jit(solution)/shard_map/dot_general | solution.py:31
  539.1 6.8 add_convert_fusion.2
  545.9 15.0 %pad_maximum_fusion = bf16[32,384,768]{2,1,0:T(8,128)(2,1)} fusion(bf16[32,96,768]{2,1,0:T(8,128)(2,1)S(1)} %bitcast.267, bf16[32,192,768]{2,1,0:T(8,128)(2,1)} %bitcast.246, bf16[32,24,768]{2,1,0:T(8,128)(2,1)} %bitcast.273, bf16[32,72,768]{2,1,0:T(8,128)(2,1)} %bitcast.268), kind=kLoop, calls=%fused_computation.2 | loop fusion | flops 75497472 | bytes 37748736 | tf_op jit(solution)/shard_map/concatenate | solution.py:277
  561.7 23.2 %all-gather.8.cloned.1.call-done = bf16[3072,768]{1,0:T(8,128)(2,1)} async-done(((bf16[384,768]{1,0:T(8,128)(2,1)}), bf16[3072,768]{1,0:T(8,128)(2,1)}) %all-gather.8.cloned.1.call-update) | async-done | bytes 4718608 | tf_op jit(solution)/shard_map/all_gather | solution.py:283
  584.9 26.8 %scatter_custom_fusion = f32[4001,768]{1,0:T(8,128)} fusion(s32[3072]{0:T(1024)S(1)} %bitcast.299, bf16[3072,768]{1,0:T(8,128)(2,1)} %all-gather.8.cloned.1.call-done, f32[]{:T(128)} %constant.64.clone.1), kind=kCustom, calls=%fused_computation.13 | custom fusion | flops 4718592 | bytes 17009668 | tf_op jit(solution)/shard_map/scatter-add | solution.py:285
  611.7 7.7 slice.532
  624.2 1.9 copy.56
  627.4 254.2 %reduce-scatter.6.cloned.1.call-done = bf16[1,384,768]{2,1,0:T(8,128)(2,1)} async-done(((bf16[32,384,768]{2,1,0:T(8,128)(2,1)}), bf16[1,384,768]{2,1,0:T(8,128)(2,1)}) %reduce-scatter.6.cloned.1.call-update) | async-done | bytes 589840 | tf_op jit(solution)/shard_map/reduce_scatter | solution.py:280
  881.6 2.0 fusion.66
  883.6 17.3 %reduce_sum.289 = bf16[4000,768]{1,0:T(8,128)(2,1)} reduce(bf16[4,4000,768]{2,1,0:T(8,128)(2,1)} %bitcast.265, bf16[]{:T(256)} %constant.84.clone.1), dimensions={0}, to_apply=%region_32.34 | reduce | flops 9216000 | bytes 30720002 | tf_op jit(solution)/shard_map/reduce_sum | solution.py:288
  900.9 6.6 fusion.2
  908.8 39.9 %all-reduce = (f32[2305]{0:T(1024)S(1)}, f32[]{:T(128)}) all-reduce(f32[2305]{0:T(1024)S(1)} %pad_maximum_fusion.18, f32[]{:T(128)S(6)} %add.363), channel_id=1, replica_groups=mesh['dp'=8,'head'=4] {'dp','head'}, use_global_device_ids=true, to_apply=%region_25.27 | all-reduce | flops 2306 | bytes 18448 | tf_op jit(solution)/shard_map/psum | solution.py:292
  952.4 2.2 fusion.71
  954.6 2.1 fusion.60
  956.7 2.0 fusion.83
  958.6 2.2 fusion.77
  960.8 2.2 add_divide_fusion.2
  968.6 2.8 fusion.183
  971.4 2.8 copy.59
  978.0 28.9 %fusion.180 = (bf16[4000,768]{1,0:T(8,128)(2,1)}, f32[4000,768]{1,0:T(8,128)}, f32[4000,768]{1,0:T(8,128)}, f32[4000,768]{1,0:T(8,128)}) fusion(f32[4000,768]{1,0:T(8,128)} %param.25, f32[]{:T(128)S(6)} %div.137, bf16[4000,768]{1,0:T(8,128)(2,1)} %reduce_sum.289, f32[4000,768]{1,0:T(8,128)} %param.26, f32[4000,768]{1,0:T(8,128)} %param.27), kind=kLoop, calls=%fused_computation.347 | loop fusion | flops 55296000 | bytes 86016000 | tf_op jit(solution)/shard_map/convert_element_type | solution.py:344
  (487 shorter events, 89.6 us)
Async XLA Ops:
  8.0 72.6 %copy-start = (s32[2,1,3]{2,1,0:T(1,128)S(1)}, s32[2,1,3]{2,1,0:T(1,128)}, u32[]{:S(2)}) copy-start(s32[2,1,3]{2,1,0:T(1,128)} %param.17) | copy-start | bytes 76
  8.0 232.8 %reduce-scatter.4.cloned.1.call-start = ((), (), s32[]{:S(2)}) async-start(), calls=%async_computation.3 | async-start | bytes 5308416 | tf_op jit(solution)/shard_map/reduce_scatter | solution.py:228
  52.0 20.4 %copy-start.94 = (s32[2,4096]{1,0:T(2,128)}, s32[2,4096]{1,0:T(2,128)S(1)}, u32[]{:S(2)}) copy-start(s32[2,4096]{1,0:T(2,128)S(1)} %all_gather.21) | copy-start | bytes 98308
  52.8 19.7 %copy-start.102 = (s32[8,1,128]{2,1,0:T(1,128)}, s32[8,1,128]{2,1,0:T(1,128)S(1)}, u32[]{:S(2)}) copy-start(s32[8,1,128]{2,1,0:T(1,128)S(1)} %get-tuple-element.169) | copy-start | bytes 12292
  52.8 19.6 %copy-start.100 = (s32[8,256]{1,0:T(8,128)}, s32[8,256]{1,0:T(8,128)S(1)}, u32[]{:S(2)}) copy-start(s32[8,256]{1,0:T(8,128)S(1)} %get-tuple-element.125) | copy-start | bytes 24580
  78.3 5.9 copy-start.105
  78.4 164.2 %all-gather.10.cloned.1.call-start = ((), (), s32[]{:S(2)}) async-start(), calls=%async_computation.7 | async-start | bytes 19464192 | tf_op jit(solution)/shard_map/all_gather | solution.py:234
  80.5 269.4 %all-gather.12.cloned.1.call-start = ((), (), s32[]{:S(2)}) async-start(), calls=%async_computation.8 | async-start | bytes 6488064 | tf_op jit(solution)/shard_map/all_gather | solution.py:230
  83.1 183.9 %copy-start.135 = (s32[128]{0:T(128)}, s32[128]{0:T(128)S(1)}, u32[]{:S(2)}) copy-start(s32[128]{0:T(128)S(1)} %iota_add_fusion.3) | copy-start | bytes 1540
  269.3 48.1 %copy-start.4 = (bf16[32,72,768]{2,1,0:T(8,128)(2,1)}, bf16[32,72,768]{2,1,0:T(8,128)(2,1)S(1)}, u32[]{:S(2)}) copy-start(bf16[32,72,768]{2,1,0:T(8,128)(2,1)S(1)} %slice.311) | copy-start | bytes 10616836
  273.5 23.3 %collective-permute-start = (bf16[256,24,64]{0,2,1:T(8,128)(2,1)}, bf16[256,24,64]{0,2,1:T(8,128)(2,1)}, u32[]{:S(2)}, u32[]{:S(2)}) collective-permute-start(bf16[256,24,64]{0,2,1:T(8,128)(2,1)} %pad_maximum_fusion.12), channel_id=1, source_target_pairs={{0,1},{1,0},{2,3},{3,2},{4,5},{5,4},{6,7},{7,6},{8,9},{9,8},{10,11... | collective-permute-start | bytes 2359304 | tf_op jit(solution)/shard_map/ppermute | solution.py:107
  275.1 47.3 %collective-permute-start.2 = (bf16[128,4096]{1,0:T(8,128)(2,1)}, bf16[128,4096]{1,0:T(8,128)(2,1)}, u32[]{:S(2)}, u32[]{:S(2)}) collective-permute-start(bf16[128,4096]{1,0:T(8,128)(2,1)} %get-tuple-element.95), channel_id=1, source_target_pairs={{0,2},{1,3},{2,0},{3,1},{4,6},{5,7},{6,4},{7,5},{8,10},{9,11},{10,... | collective-permute-start | bytes 3145736 | tf_op jit(solution)/shard_map/ppermute | solution.py:107
  281.1 222.9 %reduce-scatter.8.cloned.1.call-start = ((), (), s32[]{:S(2)}) async-start(), calls=%async_computation.5 | async-start | bytes 6488064 | tf_op jit(solution)/shard_map/reduce_scatter | solution.py:265
  301.6 5.3 slice-start
  306.2 6.1 copy-start.13
  318.7 8.1 copy-start.62
  320.9 5.9 copy-start.68
  320.9 5.8 collective-permute-start.1
  324.1 5.5 copy-start.118
  329.6 7.7 slice-start.3
  337.2 31.7 %copy-start.16 = (f32[256,768]{1,0:T(8,128)}, f32[256,768]{1,0:T(8,128)S(1)}, u32[]{:S(2)}) copy-start(f32[256,768]{1,0:T(8,128)S(1)} %get-tuple-element.151) | copy-start | bytes 2359300
  342.7 5.2 copy-start.33
  347.9 14.6 %copy-start.120 = (f32[256]{0:T(256)}, f32[256]{0:T(256)S(1)}, u32[]{:S(2)}) copy-start(f32[256]{0:T(256)S(1)} %get-tuple-element.136) | copy-start | bytes 3076
  355.7 7.0 slice-start.21
  355.7 7.0 slice-start.24
  359.9 5.3 slice-start.6
  359.9 5.4 slice-start.7
  362.7 6.2 copy-start.41
  370.1 7.8 slice-start.14
  382.9 8.0 copy-start.51
  384.2 6.8 collective-permute-start.3
  390.9 11.5 %slice-start.26 = ((s8[4718592]{0:T(1024)(128)(4,1)}), s8[524288]{0:T(1024)(128)(4,1)S(1)}, s32[]{:S(2)}) async-start(s8[4718592]{0:T(1024)(128)(4,1)} %bitcast.279), calls=%async_computation.36 | async-start | bytes 1048576
  390.9 193.9 %all-gather.8.cloned.1.call-start = ((), (), s32[]{:S(2)}) async-start(), calls=%async_computation.6 | async-start | bytes 5308416 | tf_op jit(solution)/shard_map/all_gather | solution.py:283
  393.2 9.2 slice-start.19
  395.0 7.4 slice-start.20
  395.0 7.4 slice-start.27
  400.2 5.1 slice-start.9
  402.4 6.6 copy-start.43
  409.0 8.0 slice-start.12
  422.6 2.4 collective-permute-start.4
  432.1 74.0 %copy-start.26 = (f32[256,768]{1,0:T(8,128)S(1)}, f32[256,768]{1,0:T(8,128)}, u32[]{:S(2)}) copy-start(f32[256,768]{1,0:T(8,128)} %copy-done.24) | copy-start | bytes 2359300
  432.4 75.3 %copy-start.34 = (bf16[256,3072]{1,0:T(8,128)(2,1)S(1)}, bf16[256,3072]{1,0:T(8,128)(2,1)}, u32[]{:S(2)}) copy-start(bf16[256,3072]{1,0:T(8,128)(2,1)} %copy-done.33) | copy-start | bytes 4718596
  505.8 375.8 %reduce-scatter.6.cloned.1.call-start = ((), (), s32[]{:S(2)}) async-start(), calls=%async_computation.4 | async-start | bytes 19464192 | tf_op jit(solution)/shard_map/reduce_scatter | solution.py:280
  509.8 8.3 copy-start.86
  527.6 11.5 %copy-start.38 = (bf16[1,384,768]{2,1,0:T(8,128)(2,1)S(1)}, bf16[1,384,768]{2,1,0:T(8,128)(2,1)}, u32[]{:S(2)}) copy-start(bf16[1,384,768]{2,1,0:T(8,128)(2,1)} %reduce-scatter.4.cloned.1.call-done) | copy-start | bytes 1769476
  527.6 11.5 %copy-start.53 = (bf16[256,36,64]{0,2,1:T(8,128)(2,1)S(1)}, bf16[256,36,64]{0,2,1:T(8,128)(2,1)}, u32[]{:S(2)}) copy-start(bf16[256,36,64]{0,2,1:T(8,128)(2,1)} %copy-done.52) | copy-start | bytes 3538948
  527.6 11.5 %copy-start.115 = (f32[256]{0:T(256)S(1)}, f32[256]{0:T(256)}, u32[]{:S(2)}) copy-start(f32[256]{0:T(256)} %get-tuple-element.128) | copy-start | bytes 3076
  539.1 6.8 copy-start.11
  560.9 322.6 %all-gather.14.cloned.1.call-start = ((), (), s32[]{:S(2)}) async-start(), calls=%async_computation.9 | async-start | bytes 30720000 | tf_op jit(solution)/shard_map/all_gather | solution.py:288
  621.0 5.0 copy-start.127
  621.0 5.6 copy-start.130
  621.0 5.6 copy-start.132
  621.0 5.6 copy-start.131
  621.1 5.6 copy-start.133
  621.1 5.6 copy-start.129
  900.9 62.1 %slice-start.16 = ((s8[9437184]{0:T(1024)(128)(4,1)}), s8[1048576]{0:T(1024)(128)(4,1)S(1)}, s32[]{:S(2)}) async-start(s8[9437184]{0:T(1024)(128)(4,1)} %bitcast.255), calls=%async_computation.26 | async-start | bytes 2097152
  952.4 10.6 %slice-start.17 = ((s8[9437184]{0:T(1024)(128)(4,1)}), s8[4194304]{0:T(1024)(128)(4,1)S(1)}, s32[]{:S(2)}) async-start(s8[9437184]{0:T(1024)(128)(4,1)} %bitcast.255), calls=%async_computation.27 | async-start | bytes 8388608
  968.6 5.6 copy-start.55
  971.4 5.6 copy-start.104
  971.4 5.6 copy-start.77
  978.0 28.9 %copy-start.106 = (f32[3,768]{1,0:T(4,128)S(1)}, f32[3,768]{1,0:T(4,128)}, u32[]{:S(2)}) copy-start(f32[3,768]{1,0:T(4,128)} %param.28) | copy-start | bytes 27652
  978.0 28.9 %copy-start.116 = (f32[3,768]{1,0:T(4,128)S(1)}, f32[3,768]{1,0:T(4,128)}, u32[]{:S(2)}) copy-start(f32[3,768]{1,0:T(4,128)} %param.29) | copy-start | bytes 27652
  978.0 28.9 %copy-start.117 = (f32[3,768]{1,0:T(4,128)S(1)}, f32[3,768]{1,0:T(4,128)}, u32[]{:S(2)}) copy-start(f32[3,768]{1,0:T(4,128)} %param.30) | copy-start | bytes 27652
  978.0 29.6 %copy-start.1 = (s32[2,1,3]{2,1,0:T(1,128)S(1)}, s32[2,1,3]{2,1,0:T(1,128)}, u32[]{:S(2)}) copy-start(s32[2,1,3]{2,1,0:T(1,128)} %param.17) | copy-start | bytes 76
  (113 other events, 318.6 us)
Sparse Core Ops, SparseCore 0:
  78.5 162.2 reduce-scatter.3
  505.9 78.8 all-gather.7
  619.6 150.5 all-gather.13
Sparse Core Ops, SparseCore 1:
  82.3 157.9 all-gather.9
  281.2 68.7 all-gather.11
  391.0 113.0 reduce-scatter.7
  561.0 320.5 reduce-scatter.5
